TPU v7x, 32 devices: a whole 2x2x4 slice. The times are simulated.
32 devices in a mesh: wide: 8 (over y, x, core), narrow: 4 (over z).
Axes of the slice: x: 2, y: 2, z: 4, core: 2. Of those that a mesh axis runs over, the one named last changes fastest.
Arguments:
- hidden_in: bfloat16 [131072, 768], P(('wide', 'narrow')), may hold values from -6 to 6
- lengths: int32 [256], P(('wide', 'narrow')), may hold values from 16 to 512, as said below
- labels: int32 [256], P(('wide', 'narrow')), may hold values from 0 to 2
- qkv_weight: bfloat16 [768, 2304], replicated, may hold values from -0.21875 to 0.21875
- qkv_bias: float32 [2304], replicated, may hold values from -4 to 4
- out_weight: bfloat16 [768, 768], replicated, may hold values from -0.875 to 0.875
- out_bias: float32 [768], replicated, may hold values from -4 to 4
- attention_gain: float32 [768], replicated, may hold values from 0.5 to 1.5
- attention_shift: float32 [768], replicated, may hold values from -4 to 4
- up_weight: bfloat16 [768, 3072], replicated, may hold values from -0.21875 to 0.21875
- up_bias: float32 [3072], replicated, may hold values from -4 to 4
- down_weight: bfloat16 [3072, 768], replicated, may hold values from -0.109375 to 0.109375
- down_bias: float32 [768], replicated, may hold values from -4 to 4
- output_gain: float32 [768], replicated, may hold values from 0.5 to 1.5
- output_shift: float32 [768], replicated, may hold values from -4 to 4
- pooler_weight: bfloat16 [768, 768], replicated, may hold values from -0.21875 to 0.21875
- pooler_bias: float32 [768], replicated, may hold values from -6 to 6
- ramp_weight: float32 [768, 3], replicated, may hold values from -1.5 to 1.5
- ramp_bias: float32 [3], replicated, may hold values from -6 to 6
Outputs:
- hidden_out: bfloat16 [131072, 768], P(('wide', 'narrow'))
- logits: float32 [256, 3], P(('wide', 'narrow'))
- grad_pooler_weight: float32 [768, 768], replicated
- grad_pooler_bias: float32 [768], replicated
- grad_ramp_weight: float32 [768, 3], replicated
- grad_ramp_bias: float32 [3], replicated
- entropy: float32 [], replicated
Inputs may be any that keep to these rules, and one draw needn't show every extreme that they name: `lengths`: every sequence has at least 16 tokens; in every draw some sequence fills its slot of 512.
All inputs are finite; a program needn't handle non-finite values.
Results may differ from a plain program's by a relative error of at most 0.0075.
Values sent between devices are 32-bit elements; how exact they have to be, the bound alone decides.
No kernel may reach another device: no remote copies, remote signals or barrier semaphores. Data moves between devices by JAX's collectives and lax.ppermute only.
A program may use at most 128 MiB of HBM per device.

v0:
```python
import functools

import jax
import jax.numpy as jnp
from jax import lax
from jax.experimental import pallas as pl
from jax.experimental.pallas import tpu as pltpu
from jax.sharding import PartitionSpec as P

D = 768
HEADS = 12
HEAD_DIM = 64
FF = 3072
CLASSES = 3
LANES = 128
KEY_BLOCK = 128
QUAD = 2 * LANES
GROUP = 4
EXTRA = 128
SAFE = 1e25
TILES = 2

AXES = ("wide", "narrow")
ROWS_BY_ROWS = (((1,), (1,)), ((), ()))
COLS_BY_COLS = (((0,), (0,)), ((), ()))
f32 = jnp.float32
bf16 = jnp.bfloat16


def product(left, right):
    return jnp.dot(left, right, preferred_element_type=f32)


def layer_norm(values, gain, shift):
    center = values - jnp.mean(values, axis=-1, keepdims=True)
    spread = jnp.mean(center * center, axis=-1, keepdims=True)
    return center * lax.rsqrt(spread + 1e-12) * gain + shift


def gelu(values):
    half = 0.5 * values
    return half + half * lax.erf(values * 0.7071067811865476)


def blocks_of(length):
    return (length + KEY_BLOCK - 1) // KEY_BLOCK


def project(tile, x, load_x, lengths, qkv_w, qkv_bias, table, queries, keys, values, keys_ready):
    slots, length = x.shape[0] // TILES, x.shape[1]
    per_slot = length // KEY_BLOCK

    def queries_step(step, carry):
        first = slots * tile + 2 * step
        for i in range(2):
            load_x(first + i).wait()
        tokens = x[pl.ds(first, 2)].reshape(2 * length, D)
        rows = pl.ds(pl.multiple_of(2 * length * step, 2 * length), 2 * length)
        for start in range(0, D, QUAD):
            lanes = slice(start, start + QUAD)
            found = (product(tokens, qkv_w[:, lanes]) + qkv_bias[:, lanes]).astype(bf16)
            queries[rows, lanes] = found * jnp.asarray(HEAD_DIM ** (-0.5), bf16)
        return carry

    lax.fori_loop(0, slots // 2, queries_step, 0)
    keys_ready()
    for entry in range(slots * per_slot + GROUP):
        table[entry] = 0
    total = 0
    for slot in range(slots):
        for block in range(per_slot):
            table[total + block] = slot * per_slot + block
        total = total + blocks_of(lengths[slots * tile + slot])

    def keys_step(group, carry):
        tokens = []
        for i in range(GROUP):
            entry = table[group * GROUP + i]
            row = pl.multiple_of(entry % per_slot * KEY_BLOCK, KEY_BLOCK)
            tokens.append(x[slots * tile + entry // per_slot, pl.ds(row, KEY_BLOCK), :])
        tokens = jnp.concatenate(tokens, axis=0)
        for kept, start in ((keys, D), (values, 2 * D)):
            lanes = slice(start, start + D)
            found = (product(tokens, qkv_w[:, lanes]) + qkv_bias[:, lanes]).astype(bf16)
            for i in range(GROUP):
                row = pl.multiple_of(table[group * GROUP + i] * KEY_BLOCK, KEY_BLOCK)
                kept[pl.ds(row, KEY_BLOCK), :] = found[i * KEY_BLOCK : (i + 1) * KEY_BLOCK]
        return carry

    lax.fori_loop(0, (total + GROUP - 1) // GROUP, keys_step, 0)


def two_heads(low, block):
    zero = jnp.zeros((), block.dtype)
    return jnp.concatenate([jnp.where(low, block, zero), jnp.where(low, zero, block)], axis=0)


def visible_rows(start, length):
    return start + lax.broadcasted_iota(jnp.int32, (KEY_BLOCK, LANES), 0) < length


def attend(slot, blocks, length, queries, keys, values, contexts, extremes):
    low = lax.broadcasted_iota(jnp.int32, (1, LANES), 1) < HEAD_DIM
    half = contexts[0].shape[0]
    seen = blocks * KEY_BLOCK
    base = slot * 2 * half
    visible = visible_rows(seen - KEY_BLOCK, length)
    ones = two_heads(low, jnp.ones((KEY_BLOCK, LANES), bf16))
    ones_last = two_heads(low, jnp.where(visible, 1.0, 0.0).astype(bf16))
    extreme = None
    for pair in range(0, D, LANES):
        lanes = slice(pair, pair + LANES)
        key_blocks, value_blocks = [], []
        for start in range(0, seen, KEY_BLOCK):
            rows = pl.ds(pl.multiple_of(base + start, KEY_BLOCK), KEY_BLOCK)
            value_block, counted = values[rows, lanes], ones
            if start + KEY_BLOCK == seen:
                value_block = jnp.where(visible, value_block, jnp.zeros((), bf16))
                counted = ones_last
            key_blocks.append(two_heads(low, keys[rows, lanes]))
            value_blocks.append(jnp.concatenate([two_heads(low, value_block), counted], axis=1))
        for part, context in enumerate(contexts):
            rows = pl.ds(pl.multiple_of(base + part * half, half), half)
            mine = queries[rows, lanes]
            total = None
            for key_block, value_block in zip(key_blocks, value_blocks):
                scores = lax.dot_general(mine, key_block, ROWS_BY_ROWS, preferred_element_type=f32)
                term = product(jnp.exp(scores).astype(bf16), value_block)
                total = term if total is None else total + term
            sums = total[:, LANES:]
            inverse = 1.0 / sums
            context[:, lanes] = (total[:, :LANES] * inverse).astype(bf16)
            farthest = jnp.max(jnp.maximum(sums, inverse).reshape(half // 8, 8, LANES), axis=0)
            extreme = farthest if extreme is None else jnp.maximum(extreme, farthest)
    extremes[...] = extreme


def attend_shifted(slot, length, queries, keys, values, contexts):
    low = lax.broadcasted_iota(jnp.int32, (1, LANES), 1) < HEAD_DIM
    half = contexts[0].shape[0]
    base = slot * 2 * half

    def pair_step(pair, carry):
        lanes = pl.ds(pl.multiple_of(pair * LANES, LANES), LANES)
        key_blocks, value_blocks = [], []
        for start in range(0, 2 * half, KEY_BLOCK):
            rows = pl.ds(pl.multiple_of(base + start, KEY_BLOCK), KEY_BLOCK)
            visible = visible_rows(start, length)
            key_block, value_block = keys[rows, lanes], values[rows, lanes]
            if start == 0:
                first_key = key_block[0:1, :]
            key_blocks.append(two_heads(low, jnp.where(visible, key_block, first_key)))
            value_block = jnp.where(visible, value_block, jnp.zeros((), bf16))
            counted = jnp.where(visible, 1.0, 0.0).astype(bf16)
            value_blocks.append(jnp.concatenate([two_heads(low, value_block), two_heads(low, counted)], axis=1))

        def rows_step(context, start, step):
            offset = pl.multiple_of(step * KEY_BLOCK, KEY_BLOCK)
            mine = queries[pl.ds(pl.multiple_of(base + start + offset, KEY_BLOCK), KEY_BLOCK), lanes]
            scores = [lax.dot_general(mine, block, ROWS_BY_ROWS, preferred_element_type=f32) for block in key_blocks]
            top = functools.reduce(jnp.maximum, scores)
            top_low = jnp.max(top[:, :KEY_BLOCK], axis=-1, keepdims=True)
            top_high = jnp.max(top[:, KEY_BLOCK:], axis=-1, keepdims=True)
            total = None
            for score, block in zip(scores, value_blocks):
                shifted = jnp.concatenate([score[:, :KEY_BLOCK] - top_low, score[:, KEY_BLOCK:] - top_high], axis=1)
                term = product(jnp.exp(shifted).astype(bf16), block)
                total = term if total is None else total + term
            context[pl.ds(offset, KEY_BLOCK), lanes] = (total[:, :LANES] / total[:, LANES:]).astype(bf16)

        for part, context in enumerate(contexts):

            def step(i, carry, part=part, context=context):
                rows_step(context, part * half, i)
                return carry

            lax.fori_loop(0, half // KEY_BLOCK, step, 0)
        return carry

    lax.fori_loop(0, D // LANES, pair_step, 0)


def close_attention(slot, first, x, context, out_w, vectors, after):
    out_bias, attention_gain, attention_shift = vectors
    slots, half = after.shape[0], after.shape[1]
    for j in range(slots):
        attended = product(context[j], out_w[...]) + out_bias
        tokens = x[slot + j, first : first + half, :].astype(f32)
        after[j] = layer_norm(tokens + attended, attention_gain, attention_shift)


def feed_forward(tile, up_w, down_w, vectors, active, after, result, emit=None):
    up_bias, down_bias, output_gain, output_shift = vectors
    per_tile, half = after.shape[0], after.shape[1]
    total = per_tile * half
    for chunk in range(FF // D):
        spot = slice(chunk * D, (chunk + 1) * D)
        for j in range(0, per_tile, 2):
            rows = after[j : j + 2].reshape(2 * half, D).astype(bf16)
            expanded = product(rows, up_w[:, spot]) + up_bias[:, spot]
            active[chunk * total + j * half : chunk * total + (j + 2) * half, :] = gelu(expanded).astype(bf16)
    for j in range(per_tile):
        spread = [active[chunk * total + j * half : chunk * total + (j + 1) * half, :] for chunk in range(FF // D)]
        second = product(jnp.concatenate(spread, axis=1), down_w[...]) + down_bias
        done = layer_norm(after[j] + second, output_gain, output_shift).astype(bf16)
        result[tile, j] = done
        if emit is not None:
            emit(per_tile * tile + j, done)


def vectors_of(held):
    widths = (3 * D, D, D, D, FF, D, D, D)
    return [held[i : i + 1, :width] for i, width in enumerate(widths)]


def first_kernel(lengths, labels, x_hbm, qkv_hbm, out_hbm, up_hbm, down_hbm, *rest):
    vectors_hbm = rest[:8]
    hidden_hbm, later_hbm, leads_hbm = rest[8:11]
    x, later, out_w, up_w, down_w, held, qkv_w, lead, context, table, queries, keys, values, extremes, after, active, result, load_sem, x_sem, store_sem, vector_sem, later_sem, lead_sem = rest[11:]
    slots = x.shape[0]
    per_tile, half = result.shape[1:3]

    def load_x(slot):
        return pltpu.make_async_copy(x_hbm.at[slot], x.at[slot], x_sem.at[slot])

    sources = [(qkv_hbm.at[:, spot], qkv_w.at[:, spot]) for spot in (pl.ds(0, D), pl.ds(D, 2 * D))]
    sources += [(out_hbm, out_w), (up_hbm, up_w), (down_hbm, down_w)]
    loads = [pltpu.make_async_copy(a, b, load_sem.at[i]) for i, (a, b) in enumerate(sources)]
    small = [
        pltpu.make_async_copy(ref, held.at[i, pl.ds(0, ref.shape[0])], vector_sem.at[i])
        for i, ref in enumerate(vectors_hbm)
    ]
    for copy in (loads[0], load_x(0), load_x(1), *small):
        copy.start()

    def store(tile):
        return pltpu.make_async_copy(
            result.at[tile], hidden_hbm.at[pl.ds(per_tile * tile, per_tile), pl.ds(0, half), :], store_sem.at[tile]
        )

    def store_later(slot):
        return pltpu.make_async_copy(later.at[slot], later_hbm.at[slot], later_sem.at[slot])

    for copy in (loads[0], *small):
        copy.wait()
    loads[1].start()
    for slot in range(2, slots):
        load_x(slot).start()
    vectors = vectors_of(held)

    def contexts_of(tile, j):
        return context.at[j], later.at[per_tile * tile + j]

    def attention_step(tile):
        def step(j, carry):
            length = lengths[per_tile * tile + j]
            for blocks in range(1, x.shape[1] // KEY_BLOCK + 1):

                @pl.when(blocks_of(length) == blocks)
                def _():
                    attend(j, blocks, length, queries, keys, values, contexts_of(tile, j), extremes.at[j])

            return carry

        return step

    def shifted_step(tile):
        def step(j, carry):
            length = lengths[per_tile * tile + j]
            attend_shifted(j, length, queries, keys, values, contexts_of(tile, j))
            return carry

        return step

    def emit(slot, done):
        place = lax.broadcasted_iota(jnp.int32, (1, EXTRA), 1)
        facts = jnp.where(place == 0, lengths[slot], labels[slot]).astype(f32)
        lead[pl.ds(slot, 1), :] = jnp.concatenate([done[0:1, :].astype(f32), facts], axis=1)

    def tile_step(tile, carry):
        def keys_ready():
            @pl.when(tile == 0)
            def _():
                loads[1].wait()
                for load in loads[2:]:
                    load.start()

        project(tile, x, load_x, lengths, qkv_w, vectors[0], table, queries, keys, values, keys_ready)
        lax.fori_loop(0, per_tile, attention_step(tile), 0)

        @pl.when(jnp.logical_not(jnp.max(extremes[...]) <= SAFE))
        def _():
            lax.fori_loop(0, per_tile, shifted_step(tile), 0)

        for j in range(per_tile):
            store_later(per_tile * tile + j).start()

        @pl.when(tile == 0)
        def _():
            for load in loads[2:]:
                load.wait()

        close_attention(per_tile * tile, 0, x, context, out_w, vectors[1:4], after)
        feed_forward(tile, up_w, down_w, vectors[4:], active, after, result, emit)
        store(tile).start()
        return carry

    lax.fori_loop(0, TILES, tile_step, 0)
    def each_device(act):
        def step(device, carry):
            act(pltpu.make_async_copy(lead, leads_hbm.at[device], lead_sem.at[device]))
            return carry

        lax.fori_loop(0, leads_hbm.shape[0], step, 0)

    each_device(lambda copy: copy.start())
    each_device(lambda copy: copy.wait())
    for tile in range(TILES):
        store(tile).wait()
    for slot in range(slots):
        store_later(slot).wait()


def second_kernel(x_hbm, context_hbm, out_hbm, up_hbm, down_hbm, *rest):
    vectors_hbm = rest[:8]
    hidden_in_place, hidden_hbm, x, context, out_w, up_w, down_w, held = rest[8:16]
    after, active, result, load_sem, x_sem, context_sem, store_sem, vector_sem = rest[16:]
    per_tile, half = result.shape[1:3]

    def load_rows(tile):
        spot = pl.ds(per_tile * tile, per_tile)
        return (
            pltpu.make_async_copy(context_hbm.at[spot], context.at[spot], context_sem.at[tile]),
            pltpu.make_async_copy(x_hbm.at[spot, pl.ds(half, half), :], x.at[spot], x_sem.at[tile]),
        )

    sources = [(out_hbm, out_w), (up_hbm, up_w), (down_hbm, down_w)]
    loads = [pltpu.make_async_copy(a, b, load_sem.at[i]) for i, (a, b) in enumerate(sources)]
    small = [
        pltpu.make_async_copy(ref, held.at[i, pl.ds(0, ref.shape[0])], vector_sem.at[i])
        for i, ref in enumerate(vectors_hbm)
    ]
    for copy in (loads[0], *load_rows(0), *small):
        copy.start()
    for copy in (loads[0], *load_rows(0), *small):
        copy.wait()
    for tile in range(1, TILES):
        for copy in load_rows(tile):
            copy.start()
    for load in loads[1:]:
        load.start()
    vectors = vectors_of(held)

    def store(tile):
        return pltpu.make_async_copy(
            result.at[tile], hidden_hbm.at[pl.ds(per_tile * tile, per_tile), pl.ds(half, half), :], store_sem.at[tile]
        )

    def attention_step(step, carry):
        @pl.when(step == per_tile // 2)
        def _():
            for tile in range(1, TILES):
                for copy in load_rows(tile):
                    copy.wait()

        mine = pl.ds(2 * step, 2)
        close_attention(2 * step, 0, x, context.at[mine], out_w, vectors[1:4], after.at[mine])
        return carry

    def tile_step(tile, carry):
        mine = pl.ds(per_tile * tile, per_tile)
        feed_forward(tile, up_w, down_w, vectors[4:], active, after.at[mine], result)
        store(tile).start()
        return carry

    lax.fori_loop(0, x.shape[0] // 2, attention_step, 0)
    for load in loads[1:]:
        load.wait()
    lax.fori_loop(0, TILES, tile_step, 0)
    for tile in range(TILES):
        store(tile).wait()


def ramp_kernel(gathered, pooler_w, pooler_b, ramp_t, ramp_b, logits_out, gpw_out, gpb_out, grw_out, grb_out, entropy_out, scored, found, sem):
    own = logits_out.shape[1]
    leading = gathered[:, :D].astype(bf16)
    lengths = gathered[:, D : D + 1]
    labels = gathered[:, D + 1 : D + 2]
    pooled = jnp.tanh(product(leading, pooler_w[...]) + pooler_b[...].reshape(1, -1))
    ramp = [ramp_t[c : c + 1, :] for c in range(CLASSES)]
    bias = ramp_b[...].reshape(1, -1)
    logits = [jnp.sum(pooled * ramp[c], axis=1, keepdims=True) + bias[:, c : c + 1] for c in range(CLASSES)]
    scored[...] = jnp.concatenate(logits, axis=1)
    wide, narrow = lax.axis_index(AXES[0]), lax.axis_index(AXES[1])
    place = wide * lax.axis_size(AXES[1]) + narrow
    logits_out[...] = scored[pl.ds(pl.multiple_of(place * own, own), own), :].T
    top = functools.reduce(jnp.maximum, logits)
    shifted = [one - top for one in logits]
    powers = [jnp.exp(one) for one in shifted]
    total = sum(powers[1:], powers[0])
    dlogits = [powers[c] / total - jnp.where(labels == float(c), 1.0, 0.0) for c in range(CLASSES)]
    back = sum((dlogits[c] * ramp[c] for c in range(1, CLASSES)), dlogits[0] * ramp[0])
    pooled_grad = (back * (1.0 - pooled * pooled)).astype(bf16)
    copies = []
    for i in range(D // QUAD):
        rows = slice(i * QUAD, (i + 1) * QUAD)
        found[rows, :] = lax.dot_general(leading[:, rows], pooled_grad, COLS_BY_COLS, preferred_element_type=f32)
        copies.append(pltpu.make_async_copy(found.at[rows], gpw_out.at[rows], sem.at[i]))
        copies[i].start()
    gpb_out[...] = jnp.sum(pooled_grad.astype(f32), axis=0)
    for c in range(CLASSES):
        grw_out[c : c + 1, :] = jnp.sum(pooled * dlogits[c], axis=0, keepdims=True)
    grb_out[...] = jnp.concatenate([jnp.sum(one, axis=0) for one in dlogits])
    log_total = jnp.log(total)
    log_probs = [one - log_total for one in shifted]
    row_entropy = -sum((jnp.exp(one) * one for one in log_probs[1:]), jnp.exp(log_probs[0]) * log_probs[0])
    entropy_out[...] = jnp.sum(lengths * row_entropy, axis=0, keepdims=True) / jnp.sum(lengths, axis=0, keepdims=True)
    for copy in copies:
        copy.wait()


VMEM_LIMIT = 56 * 1024 * 1024
SECOND_LIMIT = 42 * 1024 * 1024


def local(
    hidden_in, lengths, labels,
    qkv_weight, qkv_bias, out_weight, out_bias, attention_gain, attention_shift,
    up_weight, up_bias, down_weight, down_bias, output_gain, output_shift,
    pooler_weight, pooler_bias, ramp_weight, ramp_bias,
):
    slots = lengths.shape[0]
    length = hidden_in.shape[0] // slots
    half = length // 2
    rows = slots // TILES * half
    shape = (slots, length, D)
    devices = lax.axis_size(AXES)
    sequences = hidden_in.reshape(shape)
    vectors = (qkv_bias, out_bias, attention_gain, attention_shift, up_bias, down_bias, output_gain, output_shift)
    anywhere = pl.BlockSpec(memory_space=pltpu.HBM)
    in_hbm = lambda array: pltpu.with_memory_space_constraint(array, pltpu.HBM)
    scalars = pl.BlockSpec(memory_space=pltpu.SMEM)
    vmem = pl.BlockSpec(memory_space=pltpu.VMEM)
    dma = pltpu.SemaphoreType.DMA
    weights = [pltpu.VMEM(one, bf16) for one in ((D, D), (D, FF), (FF, D))]
    weights = weights + [pltpu.VMEM((len(vectors), FF), f32)]
    common = [
        pltpu.VMEM((rows * FF // D, D), bf16),
        pltpu.VMEM((TILES, slots // TILES, half, D), bf16),
    ]
    cost = pl.CostEstimate(
        flops=2 * slots * half * D * (2 * D + 2 * FF + 2 * length), bytes_accessed=30_000_000, transcendentals=0
    )
    params = pltpu.CompilerParams(vmem_limit_bytes=VMEM_LIMIT)
    hidden, later, leads = pl.pallas_call(
        first_kernel,
        name="first_half",
        out_shape=[
            pltpu.HBM(shape, bf16),
            pltpu.HBM((slots, half, D), bf16),
            pltpu.HBM((devices, slots, D + EXTRA), f32),
        ],
        in_specs=[scalars] * 2 + [anywhere] * 13,
        out_specs=[anywhere] * 3,
        scratch_shapes=[pltpu.VMEM(shape, bf16), pltpu.VMEM((slots, half, D), bf16)]
        + weights
        + [
            pltpu.VMEM((D, 3 * D), bf16),
            pltpu.VMEM((slots, D + EXTRA), f32),
            pltpu.VMEM((slots // TILES, half, D), bf16),
            pltpu.SMEM((slots // TILES * length // KEY_BLOCK + GROUP,), jnp.int32),
            pltpu.VMEM((2 * rows, D), bf16),
            pltpu.VMEM((2 * rows, D), bf16),
            pltpu.VMEM((2 * rows, D), bf16),
            pltpu.VMEM((slots // TILES, 8, LANES), f32),
        ]
        + [pltpu.VMEM((slots // TILES, half, D), f32)]
        + common
        + [dma((5,)), dma((slots,)), dma((TILES,)), dma((len(vectors),)), dma((slots,)), dma((devices,))],
        compiler_params=params,
        cost_estimate=cost,
    )(lengths, labels, *[in_hbm(a) for a in (sequences, qkv_weight, out_weight, up_weight, down_weight, *vectors)])
    gathered = lax.all_to_all(leads, AXES, 0, 0).reshape(devices * slots, D + EXTRA)
    hidden = pl.pallas_call(
        second_kernel,
        name="second_half",
        out_shape=pltpu.HBM(shape, bf16),
        in_specs=[anywhere] * 14,
        out_specs=anywhere,
        scratch_shapes=[pltpu.VMEM((slots, half, D), bf16)] * 2
        + weights
        + [pltpu.VMEM((slots, half, D), f32)]
        + common
        + [dma((3,)), dma((TILES,)), dma((TILES,)), dma((TILES,)), dma((len(vectors),))],
        input_output_aliases={13: 0},
        compiler_params=pltpu.CompilerParams(vmem_limit_bytes=SECOND_LIMIT),
        cost_estimate=cost,
    )(*[in_hbm(a) for a in (sequences, later, out_weight, up_weight, down_weight, *vectors, hidden)])
    one = lambda *shape: jax.ShapeDtypeStruct(shape, f32)
    logits, gpw, gpb, grw, grb, entropy = pl.pallas_call(
        ramp_kernel,
        name="off_ramp",
        out_shape=[one(CLASSES, slots), pltpu.HBM((D, D), f32), one(D), one(CLASSES, D), one(CLASSES), one(1, 1)],
        in_specs=[vmem] * 5,
        out_specs=[vmem, anywhere] + [vmem] * 4,
        scratch_shapes=[pltpu.VMEM((devices * slots, CLASSES), f32), pltpu.VMEM((D, D), f32), dma((D // QUAD,))],
        compiler_params=pltpu.CompilerParams(vmem_limit_bytes=8 * 1024 * 1024 + 5 * 4 * gathered.size),
    )(gathered, pooler_weight, pooler_bias, ramp_weight.T, ramp_bias)
    return hidden.reshape(hidden_in.shape), logits.T, gpw, gpb, grw.T, grb, entropy.reshape(())


def solution(mesh):
    spread = P(AXES)
    placed = (P(AXES, None), spread, spread) + (P(),) * 16
    return jax.shard_map(
        local,
        mesh=mesh,
        in_specs=placed,
        out_specs=(P(AXES, None), P(AXES, None), P(), P(), P(), P(), P()),
        check_vma=False,
    )
```

profile of v0, /device:TPU:0, one launch (start us, length us, event | category | flops | bytes accessed | tf_op | source)
XLA Modules:
  0.0 106.7 jit_solution(1294146552087164349)
XLA Ops:
  0.6 46.2 %first_half.1 = (bf16[8,512,768]{2,1,0:T(8,128)(2,1)}, bf16[8,256,768]{2,1,0:T(8,128)(2,1)}, f32[32,8,896]{2,1,0:T(8,128)}) custom-call(s32[8]{0:T(128)} %lengths.1, s32[8]{0:T(128)} %labels.1, bf16[8,512,768]{2,1,0:T(8,128)(2,1)} %bitcast.9, bf16[768,2304]{1,0:T(8,128)(2,1)} %qkv_hbm.1, bf16[768,768]{1,0:T(8,128)(2,1)} %out_hbm.3, ...), custom_call_target="tpu_custom_call" | custom-call | flops 27380416512 | bytes 30000000 | tf_op jit(solution)/shard_map/first_half/pallas_call | solution.py:455
  46.9 25.5 %all-to-all-start = ((f32[32,8,896]{2,1,0:T(8,128)}), f32[32,8,896]{2,1,0:T(8,128)S(1)}, u32[]{:S(2)}, u32[]{:S(2)}) async-start(f32[32,8,896]{2,1,0:T(8,128)} %get-tuple-element.18), calls=%async_computation | async-start | bytes 1835008 | tf_op jit(solution)/shard_map/all_to_all | solution.py:483
  72.4 0.0 copy-start
  72.4 0.0 copy-start.1
  72.4 0.0 copy-start.2
  72.4 0.0 copy-start.3
  72.5 30.4 %second_half.1 = bf16[8,512,768]{2,1,0:T(8,128)(2,1)} custom-call(bf16[8,512,768]{2,1,0:T(8,128)(2,1)} %bitcast.10, bf16[8,256,768]{2,1,0:T(8,128)(2,1)} %get-tuple-element.16.context_hbm, bf16[768,768]{1,0:T(8,128)(2,1)} %out_hbm.3, bf16[768,3072]{1,0:T(8,128)(2,1)} %up_hbm.3, bf16[3072,768]{1,0:T(8,128)(2,1)} %down_hbm.3, ...), custom_call_target="tpu_custom_call", output_to_operand_aliasing={{}: (13, {})} | custom-call | flops 27380416512 | bytes 30000000 | tf_op jit(solution)/shard_map/second_half/pallas_call | solution.py:484
  102.8 0.0 all-to-all-done
  102.8 0.0 copy-done
  102.9 0.0 copy-done.1
  102.9 0.0 copy-done.2
  102.9 0.0 copy-done.3
  102.9 3.7 %off_ramp.1 = (f32[3,8]{1,0:T(4,128)}, f32[768,768]{1,0:T(8,128)}, f32[768]{0:T(1024)}, f32[3,768]{1,0:T(4,128)}, f32[3]{0:T(128)}, /*index=5*/f32[1,1]{1,0:T(1,128)}) custom-call(f32[256,896]{1,0:T(8,128)S(1)} %bitcast.7, bf16[768,768]{1,0:T(8,128)(2,1)S(1)} %copy-done, f32[768]{0:T(1024)S(1)} %copy-done.2, f32[3,768]{1,0:T(4,128)S(1)} %bitcast.8, ...), custom_call_target="tpu_custom_call" | custom-call | tf_op jit(solution)/shard_map/off_ramp/pallas_call | solution.py:500
Async XLA Ops:
  46.9 56.0 %all-to-all-start = ((f32[32,8,896]{2,1,0:T(8,128)}), f32[32,8,896]{2,1,0:T(8,128)S(1)}, u32[]{:S(2)}, u32[]{:S(2)}) async-start(f32[32,8,896]{2,1,0:T(8,128)} %get-tuple-element.18), calls=%async_computation | async-start | bytes 1835008 | tf_op jit(solution)/shard_map/all_to_all | solution.py:483
  72.4 30.4 %copy-start = (bf16[768,768]{1,0:T(8,128)(2,1)S(1)}, bf16[768,768]{1,0:T(8,128)(2,1)}, u32[]{:S(2)}) copy-start(bf16[768,768]{1,0:T(8,128)(2,1)} %pooler_w.1) | copy-start | bytes 3538948
  72.4 30.4 %copy-start.1 = (f32[768,3]{0,1:T(4,128)S(1)}, f32[768,3]{0,1:T(4,128)}, u32[]{:S(2)}) copy-start(f32[768,3]{0,1:T(4,128)} %param.36) | copy-start | bytes 27652
  72.4 30.4 %copy-start.2 = (f32[768]{0:T(1024)S(1)}, f32[768]{0:T(1024)}, u32[]{:S(2)}) copy-start(f32[768]{0:T(1024)} %pooler_b.1) | copy-start | bytes 9220
  72.4 30.4 %copy-start.3 = (f32[3]{0:T(128)S(1)}, f32[3]{0:T(128)}, u32[]{:S(2)}) copy-start(f32[3]{0:T(128)} %ramp_b.1) | copy-start | bytes 40
where the time goes:
time: 106 us; the launch traced here: 107 us
  Pallas kernels  80.3 us (76%)
  starting transfers between devices  25.5 us (24%)
    pallas_call x1, Pallas kernels, local(): pl.pallas_call(first_kernel, name='first_half', out_shape=[pltpu.HBM(shap...  46.2 us
    pallas_call x1, Pallas kernels, local(): pl.pallas_call(second_kernel, name='second_half', out_shape=pltpu.HBM(sha...  30.4 us
    all_to_all x1, starting transfers between devices, local(): lax.all_to_all(leads, AXES, 0, 0).reshape(devices * slots, D + EXTRA)  25.5 us
    pallas_call x1, Pallas kernels, local(): pl.pallas_call(ramp_kernel, name='off_ramp', out_shape=[one(CLASSES, slot...  3.68 us
  transfers between devices with their start and end apart: 1, of which 0 were waited for; matrix products, arithmetic and copies ran while one was open for 0% of the time, Pallas kernels for 28%

commit v1 on v0

--- a/solution.py
+++ b/solution.py
@@ -203,7 +203,7 @@
         spread = [active[chunk * total + j * half : chunk * total + (j + 1) * half, :] for chunk in range(FF // D)]
         second = product(jnp.concatenate(spread, axis=1), down_w[...]) + down_bias
         done = layer_norm(after[j] + second, output_gain, output_shift).astype(bf16)
-        result[tile, j] = done
+        result[per_tile * tile + j] = done
         if emit is not None:
             emit(per_tile * tile + j, done)
 
@@ -215,10 +215,11 @@
 
 def first_kernel(lengths, labels, x_hbm, qkv_hbm, out_hbm, up_hbm, down_hbm, *rest):
     vectors_hbm = rest[:8]
-    hidden_hbm, later_hbm, leads_hbm = rest[8:11]
-    x, later, out_w, up_w, down_w, held, qkv_w, lead, context, table, queries, keys, values, extremes, after, active, result, load_sem, x_sem, store_sem, vector_sem, later_sem, lead_sem = rest[11:]
+    hidden_hbm, later_hbm, leads_hbm, out_w, held = rest[8:13]
+    x, later, up_w, down_w, qkv_w, lead, context, table, queries, keys, values, extremes, after, active, result, load_sem, x_sem, store_sem, vector_sem, later_sem, lead_sem = rest[13:]
     slots = x.shape[0]
-    per_tile, half = result.shape[1:3]
+    half = result.shape[1]
+    per_tile = result.shape[0] // TILES
 
     def load_x(slot):
         return pltpu.make_async_copy(x_hbm.at[slot], x.at[slot], x_sem.at[slot])
@@ -233,10 +234,8 @@
     for copy in (loads[0], load_x(0), load_x(1), *small):
         copy.start()
 
-    def store(tile):
-        return pltpu.make_async_copy(
-            result.at[tile], hidden_hbm.at[pl.ds(per_tile * tile, per_tile), pl.ds(0, half), :], store_sem.at[tile]
-        )
+    def store(slot):
+        return pltpu.make_async_copy(result.at[slot], hidden_hbm.at[slot, pl.ds(0, half), :], store_sem.at[slot])
 
     def store_later(slot):
         return pltpu.make_async_copy(later.at[slot], later_hbm.at[slot], later_sem.at[slot])
@@ -273,6 +272,7 @@
         return step
 
     def emit(slot, done):
+        store(slot).start()
         place = lax.broadcasted_iota(jnp.int32, (1, EXTRA), 1)
         facts = jnp.where(place == 0, lengths[slot], labels[slot]).astype(f32)
         lead[pl.ds(slot, 1), :] = jnp.concatenate([done[0:1, :].astype(f32), facts], axis=1)
@@ -302,7 +302,6 @@
 
         close_attention(per_tile * tile, 0, x, context, out_w, vectors[1:4], after)
         feed_forward(tile, up_w, down_w, vectors[4:], active, after, result, emit)
-        store(tile).start()
         return carry
 
     lax.fori_loop(0, TILES, tile_step, 0)
@@ -315,70 +314,59 @@
 
     each_device(lambda copy: copy.start())
     each_device(lambda copy: copy.wait())
-    for tile in range(TILES):
-        store(tile).wait()
     for slot in range(slots):
+        store(slot).wait()
         store_later(slot).wait()
 
 
-def second_kernel(x_hbm, context_hbm, out_hbm, up_hbm, down_hbm, *rest):
-    vectors_hbm = rest[:8]
-    hidden_in_place, hidden_hbm, x, context, out_w, up_w, down_w, held = rest[8:16]
-    after, active, result, load_sem, x_sem, context_sem, store_sem, vector_sem = rest[16:]
-    per_tile, half = result.shape[1:3]
-
-    def load_rows(tile):
-        spot = pl.ds(per_tile * tile, per_tile)
+def second_kernel(
+    x_hbm, context_hbm, up_hbm, down_hbm, out_w, held, hidden_in_place, hidden_hbm,
+    x, context, up_w, down_w, after, active, result, load_sem, x_sem, context_sem, store_sem,
+):
+    slots, half = result.shape[:2]
+    per_tile = slots // TILES
+    vectors = vectors_of(held)
+
+    def load_rows(step):
+        spot = pl.ds(2 * step, 2)
         return (
-            pltpu.make_async_copy(context_hbm.at[spot], context.at[spot], context_sem.at[tile]),
-            pltpu.make_async_copy(x_hbm.at[spot, pl.ds(half, half), :], x.at[spot], x_sem.at[tile]),
+            pltpu.make_async_copy(context_hbm.at[spot], context.at[spot], context_sem.at[step]),
+            pltpu.make_async_copy(x_hbm.at[spot, pl.ds(half, half), :], x.at[spot], x_sem.at[step]),
         )
 
-    sources = [(out_hbm, out_w), (up_hbm, up_w), (down_hbm, down_w)]
+    sources = [(up_hbm, up_w), (down_hbm, down_w)]
     loads = [pltpu.make_async_copy(a, b, load_sem.at[i]) for i, (a, b) in enumerate(sources)]
-    small = [
-        pltpu.make_async_copy(ref, held.at[i, pl.ds(0, ref.shape[0])], vector_sem.at[i])
-        for i, ref in enumerate(vectors_hbm)
-    ]
-    for copy in (loads[0], *load_rows(0), *small):
+    for copy in load_rows(0):
         copy.start()
-    for copy in (loads[0], *load_rows(0), *small):
-        copy.wait()
-    for tile in range(1, TILES):
-        for copy in load_rows(tile):
+    for step in range(1, slots // 2):
+        for copy in load_rows(step):
             copy.start()
-    for load in loads[1:]:
+    for load in loads:
         load.start()
-    vectors = vectors_of(held)
-
-    def store(tile):
+
+    def store(slot):
         return pltpu.make_async_copy(
-            result.at[tile], hidden_hbm.at[pl.ds(per_tile * tile, per_tile), pl.ds(half, half), :], store_sem.at[tile]
+            result.at[slot], hidden_hbm.at[slot, pl.ds(half, half), :], store_sem.at[slot]
         )
 
     def attention_step(step, carry):
-        @pl.when(step == per_tile // 2)
-        def _():
-            for tile in range(1, TILES):
-                for copy in load_rows(tile):
-                    copy.wait()
-
+        for copy in load_rows(step):
+            copy.wait()
         mine = pl.ds(2 * step, 2)
         close_attention(2 * step, 0, x, context.at[mine], out_w, vectors[1:4], after.at[mine])
         return carry
 
     def tile_step(tile, carry):
         mine = pl.ds(per_tile * tile, per_tile)
-        feed_forward(tile, up_w, down_w, vectors[4:], active, after.at[mine], result)
-        store(tile).start()
+        feed_forward(tile, up_w, down_w, vectors[4:], active, after.at[mine], result, lambda slot, _: store(slot).start())
         return carry
 
-    lax.fori_loop(0, x.shape[0] // 2, attention_step, 0)
-    for load in loads[1:]:
+    lax.fori_loop(0, slots // 2, attention_step, 0)
+    for load in loads:
         load.wait()
     lax.fori_loop(0, TILES, tile_step, 0)
-    for tile in range(TILES):
-        store(tile).wait()
+    for slot in range(slots):
+        store(slot).wait()
 
 
 def ramp_kernel(gathered, pooler_w, pooler_b, ramp_t, ramp_b, logits_out, gpw_out, gpb_out, grw_out, grb_out, entropy_out, scored, found, sem):
@@ -442,26 +430,27 @@
     scalars = pl.BlockSpec(memory_space=pltpu.SMEM)
     vmem = pl.BlockSpec(memory_space=pltpu.VMEM)
     dma = pltpu.SemaphoreType.DMA
-    weights = [pltpu.VMEM(one, bf16) for one in ((D, D), (D, FF), (FF, D))]
-    weights = weights + [pltpu.VMEM((len(vectors), FF), f32)]
+    weights = [pltpu.VMEM(one, bf16) for one in ((D, FF), (FF, D))]
     common = [
         pltpu.VMEM((rows * FF // D, D), bf16),
-        pltpu.VMEM((TILES, slots // TILES, half, D), bf16),
+        pltpu.VMEM((slots, half, D), bf16),
     ]
     cost = pl.CostEstimate(
         flops=2 * slots * half * D * (2 * D + 2 * FF + 2 * length), bytes_accessed=30_000_000, transcendentals=0
     )
     params = pltpu.CompilerParams(vmem_limit_bytes=VMEM_LIMIT)
-    hidden, later, leads = pl.pallas_call(
+    hidden, later, leads, *kept = pl.pallas_call(
         first_kernel,
         name="first_half",
         out_shape=[
             pltpu.HBM(shape, bf16),
             pltpu.HBM((slots, half, D), bf16),
             pltpu.HBM((devices, slots, D + EXTRA), f32),
+            pltpu.VMEM((D, D), bf16),
+            pltpu.VMEM((len(vectors), FF), f32),
         ],
         in_specs=[scalars] * 2 + [anywhere] * 13,
-        out_specs=[anywhere] * 3,
+        out_specs=[anywhere] * 3 + [vmem] * 2,
         scratch_shapes=[pltpu.VMEM(shape, bf16), pltpu.VMEM((slots, half, D), bf16)]
         + weights
         + [
@@ -476,7 +465,7 @@
         ]
         + [pltpu.VMEM((slots // TILES, half, D), f32)]
         + common
-        + [dma((5,)), dma((slots,)), dma((TILES,)), dma((len(vectors),)), dma((slots,)), dma((devices,))],
+        + [dma((5,)), dma((slots,)), dma((slots,)), dma((len(vectors),)), dma((slots,)), dma((devices,))],
         compiler_params=params,
         cost_estimate=cost,
     )(lengths, labels, *[in_hbm(a) for a in (sequences, qkv_weight, out_weight, up_weight, down_weight, *vectors)])
@@ -485,17 +474,21 @@
         second_kernel,
         name="second_half",
         out_shape=pltpu.HBM(shape, bf16),
-        in_specs=[anywhere] * 14,
+        in_specs=[anywhere] * 4 + [vmem] * 2 + [anywhere],
         out_specs=anywhere,
         scratch_shapes=[pltpu.VMEM((slots, half, D), bf16)] * 2
         + weights
         + [pltpu.VMEM((slots, half, D), f32)]
         + common
-        + [dma((3,)), dma((TILES,)), dma((TILES,)), dma((TILES,)), dma((len(vectors),))],
-        input_output_aliases={13: 0},
+        + [dma((2,)), dma((slots // 2,)), dma((slots // 2,)), dma((slots,))],
+        input_output_aliases={6: 0},
         compiler_params=pltpu.CompilerParams(vmem_limit_bytes=SECOND_LIMIT),
         cost_estimate=cost,
-    )(*[in_hbm(a) for a in (sequences, later, out_weight, up_weight, down_weight, *vectors, hidden)])
+    )(
+        *[in_hbm(a) for a in (sequences, later, up_weight, down_weight)],
+        *[pltpu.with_memory_space_constraint(a, pltpu.VMEM) for a in kept],
+        in_hbm(hidden),
+    )
     one = lambda *shape: jax.ShapeDtypeStruct(shape, f32)
     logits, gpw, gpb, grw, grb, entropy = pl.pallas_call(
         ramp_kernel,

time: 106 us -> 106 us (level)
  starting transfers between devices: 25.5 us -> 28.6 us
  Pallas kernels: 80.3 us -> 77.7 us
    all_to_all x1, starting transfers between devices: 25.5 us -> 28.6 us  [local(): lax.all_to_all(leads, AXES, 0, 0).reshape(devices * slots, D + EXTRA)]
    pallas_call x1, Pallas kernels: 30.4 us -> 28 us  [local(): pl.pallas_call(second_kernel, name='second_half', out_shape=pltpu.HBM(sha...]
  transfers between devices with their start and end apart: 1 -> 1, of which waited for: 0 -> 0; matrix products, arithmetic and copies ran while one was open for 0% -> 0% of each run, Pallas kernels for 28% -> 26%
where the time goes in v1:
time: 106 us; the launch traced here: 107 us
  Pallas kernels  77.7 us (73%)
  starting transfers between devices  28.6 us (27%)
    pallas_call x1, Pallas kernels, local(): pl.pallas_call(first_kernel, name='first_half', out_shape=[pltpu.HBM(shap...  46.1 us
    all_to_all x1, starting transfers between devices, local(): lax.all_to_all(leads, AXES, 0, 0).reshape(devices * slots, D + EXTRA)  28.6 us
    pallas_call x1, Pallas kernels, local(): pl.pallas_call(second_kernel, name='second_half', out_shape=pltpu.HBM(sha...  28 us
    pallas_call x1, Pallas kernels, local(): pl.pallas_call(ramp_kernel, name='off_ramp', out_shape=[one(CLASSES, slot...  3.67 us
  transfers between devices with their start and end apart: 1, of which 0 were waited for; matrix products, arithmetic and copies ran while one was open for 0% of the time, Pallas kernels for 26%

profile of v1, /device:TPU:0, one launch (start us, length us, event | category | flops | bytes accessed | tf_op | source)
XLA Modules:
  0.0 107.2 jit_solution(13562782586742255942)
XLA Ops:
  0.6 46.1 %first_half.1 = (bf16[8,512,768]{2,1,0:T(8,128)(2,1)}, bf16[8,256,768]{2,1,0:T(8,128)(2,1)}, f32[32,8,896]{2,1,0:T(8,128)}, bf16[768,768]{1,0:T(8,128)(2,1)S(1)}, f32[8,3072]{1,0:T(8,128)S(1)}) custom-call(s32[8]{0:T(128)} %lengths.1, s32[8]{0:T(128)} %labels.1, bf16[8,512,768]{2,1,0:T(8,128)(2,1)} %bitcast.9, bf16[768,2304]{1,0:T(8,128)(2,1)} %qkv_hbm.1, ...), custom_call_target="tpu_custom_call" | custom-call | flops 27380416512 | bytes 30000000 | tf_op jit(solution)/shard_map/first_half/pallas_call | solution.py:442
  46.7 28.6 %all-to-all-start = ((f32[32,8,896]{2,1,0:T(8,128)}), f32[32,8,896]{2,1,0:T(8,128)S(1)}, u32[]{:S(2)}, u32[]{:S(2)}) async-start(f32[32,8,896]{2,1,0:T(8,128)} %get-tuple-element.22), calls=%async_computation | async-start | bytes 1835008 | tf_op jit(solution)/shard_map/all_to_all | solution.py:472
  75.3 0.0 copy-start
  75.3 0.0 copy-start.1
  75.3 0.0 copy-start.2
  75.3 0.0 copy-start.3
  75.3 28.0 %second_half.1 = bf16[8,512,768]{2,1,0:T(8,128)(2,1)} custom-call(bf16[8,512,768]{2,1,0:T(8,128)(2,1)} %bitcast.10, bf16[8,256,768]{2,1,0:T(8,128)(2,1)} %get-tuple-element.18.context_hbm, bf16[768,3072]{1,0:T(8,128)(2,1)} %up_hbm.3, bf16[3072,768]{1,0:T(8,128)(2,1)} %down_hbm.3, ...), custom_call_target="tpu_custom_call", output_to_operand_aliasing={{}: (6, {})} | custom-call | flops 27380416512 | bytes 30000000 | tf_op jit(solution)/shard_map/second_half/pallas_call | solution.py:473
  103.3 0.0 all-to-all-done
  103.3 0.0 copy-done
  103.3 0.0 copy-done.1
  103.3 0.0 copy-done.2
  103.3 0.0 copy-done.3
  103.3 3.7 %off_ramp.1 = (f32[3,8]{1,0:T(4,128)}, f32[768,768]{1,0:T(8,128)}, f32[768]{0:T(1024)}, f32[3,768]{1,0:T(4,128)}, f32[3]{0:T(128)}, /*index=5*/f32[1,1]{1,0:T(1,128)}) custom-call(f32[256,896]{1,0:T(8,128)S(1)} %bitcast.7, bf16[768,768]{1,0:T(8,128)(2,1)S(1)} %copy-done, f32[768]{0:T(1024)S(1)} %copy-done.2, f32[3,768]{1,0:T(4,128)S(1)} %bitcast.8, ...), custom_call_target="tpu_custom_call" | custom-call | tf_op jit(solution)/shard_map/off_ramp/pallas_call | solution.py:493
Async XLA Ops:
  46.7 56.6 %all-to-all-start = ((f32[32,8,896]{2,1,0:T(8,128)}), f32[32,8,896]{2,1,0:T(8,128)S(1)}, u32[]{:S(2)}, u32[]{:S(2)}) async-start(f32[32,8,896]{2,1,0:T(8,128)} %get-tuple-element.22), calls=%async_computation | async-start | bytes 1835008 | tf_op jit(solution)/shard_map/all_to_all | solution.py:472
  75.3 28.0 %copy-start = (bf16[768,768]{1,0:T(8,128)(2,1)S(1)}, bf16[768,768]{1,0:T(8,128)(2,1)}, u32[]{:S(2)}) copy-start(bf16[768,768]{1,0:T(8,128)(2,1)} %pooler_w.1) | copy-start | bytes 3538948
  75.3 28.0 %copy-start.1 = (f32[768,3]{0,1:T(4,128)S(1)}, f32[768,3]{0,1:T(4,128)}, u32[]{:S(2)}) copy-start(f32[768,3]{0,1:T(4,128)} %param.36) | copy-start | bytes 27652
  75.3 28.0 %copy-start.2 = (f32[768]{0:T(1024)S(1)}, f32[768]{0:T(1024)}, u32[]{:S(2)}) copy-start(f32[768]{0:T(1024)} %pooler_b.1) | copy-start | bytes 9220
  75.3 28.0 %copy-start.3 = (f32[3]{0:T(128)S(1)}, f32[3]{0:T(128)}, u32[]{:S(2)}) copy-start(f32[3]{0:T(128)} %ramp_b.1) | copy-start | bytes 40
